TPU v7x, 32 devices: a whole 2x2x4 slice. The times are simulated.
32 devices in a mesh: col: 4 (over y, core), row: 8 (over z, x).
Axes of the slice: x: 2, y: 2, z: 4, core: 2. Of those that a mesh axis runs over, the one named last changes fastest.
Arguments:
- panel: bfloat16 [8, 48, 512, 128], P('row', 'col'), may hold values from -6 to 6
- stiffness: bfloat16 [8, 48, 512, 512], P('row', 'col'), may hold values from -0.25 to 0.25
- mass: float32 [8, 48, 512], P('row', 'col'), may hold values from 0.2 to 2
- resident: bfloat16 [8, 24576, 1024], P('row', None, 'col'), may hold values from -0.01953125 to 0.01953125
- face_rows: int32 [8, 2, 2048], P('row'), may hold values from 0 to 24575, as said below
- counts: int32 [8], P('row'), may hold values from 24 to 48, as said below
Outputs:
- gram: float32 [1024, 128], P(('col', 'row'))
Inputs may be any that keep to these rules, and one draw needn't show every extreme that they name: `counts`: each partition has between 24 and 48 live elements in its first slots; some partition has exactly 48. `face_rows`: each list of a partition holds 2048 distinct node rows of its live elements; its list 0 includes its last live node row.
All inputs are finite; a program needn't handle non-finite values.
Results may differ from a plain program's by a relative error of at most 0.0034.
Values may be sent and summed in bfloat16 or wider, within the bound.
A program may use at most 128 MiB of HBM per device.

v0:
```python
import jax
import jax.numpy as jnp
from jax import lax
from jax.sharding import PartitionSpec as P


def passed_along(value, axis, steps):
    count = lax.axis_size(axis)
    leading, last = (max(0, -steps), min(count, count - steps))
    return lax.ppermute(value, axis, [(source, source + steps) for source in range(leading, last)])


def shards(panel, stiffness, mass, resident, face_rows, counts):
    slots = panel.shape[1]
    nodes = panel.shape[2]
    width = panel.shape[3]
    column = lax.axis_index("col")
    slot_ids = column * slots + jnp.arange(slots, dtype=jnp.int32)
    live = slot_ids < counts[0]
    values = panel[0]
    applied = jnp.einsum("enm,ems->ens", stiffness[0], values, preferred_element_type=jnp.float32)
    applied = applied + mass[0][:, :, None] * values.astype(jnp.float32)
    applied = jnp.where(live[:, None, None], applied, 0.0).astype(jnp.bfloat16)
    local_rows = applied.reshape(slots * nodes, width)
    whole = lax.all_gather(local_rows, "col", axis=0, tiled=True)
    prev_rows = face_rows[0, 0]
    next_rows = face_rows[0, 1]
    from_next = passed_along(whole[prev_rows], "row", -1)
    from_prev = passed_along(whole[next_rows], "row", 1)
    summed = whole.astype(jnp.float32)
    summed = summed.at[next_rows].add(from_next.astype(jnp.float32))
    summed = summed.at[prev_rows].add(from_prev.astype(jnp.float32))
    summed = summed.astype(jnp.bfloat16)
    columns = resident[0]
    contract = (((0,), (0,)), ((), ()))
    own_rows = columns.shape[1] // lax.axis_size("row")
    partial_gram = lax.dot_general(columns, summed, contract, preferred_element_type=jnp.float32)
    full_gram = lax.psum(partial_gram, "row")
    gram = lax.dynamic_slice_in_dim(full_gram, lax.axis_index("row") * own_rows, own_rows, 0)
    return gram


def solution(mesh):
    in_specs = (
        P("row", "col", None, None),
        P("row", "col", None, None),
        P("row", "col", None),
        P("row", None, "col"),
        P("row", None, None),
        P("row"),
    )
    out_specs = P(("col", "row"), None)
    return jax.shard_map(shards, mesh=mesh, in_specs=in_specs, out_specs=out_specs, check_vma=False)
```

profile of v0, /device:TPU:0, one launch (start us, length us, event | category | flops | bytes accessed | tf_op | source)
XLA Modules:
  0.0 223.6 jit_solution(14641089613131606181)
XLA Ops:
  6.5 0.0 all-gather.2.cloned.1.call-start
  7.2 0.7 copy.11
  7.9 0.0 copy-start
  7.9 6.7 %select_convert_fusion = bf16[12,512,128]{2,1,0:T(8,128)(2,1)} fusion(bf16[1,12,512,512]{3,2,1,0:T(8,128)(2,1)} %param.7, bf16[1,12,512,128]{3,2,1,0:T(8,128)(2,1)} %param.6, f32[12,512]{1,0:T(8,128)S(1)} %bitcast.28, pred[12]{0:T(512)(128)(4,1)S(1)} %add_compare_fusion), kind=kOutput, calls=%fused_computation.9 | convolution fusion | flops 809238528 | bytes 9461772 | tf_op jit(solution)/shard_map/enm,ems->ens/dot_general | solution.py:21
  14.6 0.0 all-gather.2.cloned.1.call-update
  14.6 0.0 all-reduce.2.cloned.1.call-start
  14.7 0.0 copy-done
  14.7 49.1 %all-gather.2.cloned.1.call-done = bf16[24576,128]{1,0:T(8,128)(2,1)} async-done(((bf16[6144,128]{1,0:T(8,128)(2,1)}), bf16[24576,128]{1,0:T(8,128)(2,1)}) %all-gather.2.cloned.1.call-update) | async-done | bytes 6291472 | tf_op jit(solution)/shard_map/all_gather | solution.py:25
  63.9 9.2 %gather_fusion = bf16[2048,128]{1,0:T(8,128)(2,1)S(1)} fusion(bf16[24576,128]{1,0:T(8,128)(2,1)} %all-gather.2.cloned.1.call-done, s32[2048]{0:T(1024)S(1)} %broadcast_clamp_fusion.1), kind=kCustom, calls=%fused_computation | custom fusion | bytes 1056768 | tf_op jit(solution)/shard_map/gather | solution.py:28
  73.1 1.3 collective-permute-start
  74.4 9.2 %gather_fusion.1 = bf16[2048,128]{1,0:T(8,128)(2,1)S(1)} fusion(bf16[24576,128]{1,0:T(8,128)(2,1)} %all-gather.2.cloned.1.call-done, s32[2048]{0:T(1024)S(1)} %broadcast_clamp_fusion), kind=kCustom, calls=%fused_computation.1 | custom fusion | bytes 1056768 | tf_op jit(solution)/shard_map/gather | solution.py:29
  83.6 4.6 %collective-permute-start.1 = (bf16[2048,128]{1,0:T(8,128)(2,1)S(1)}, bf16[2048,128]{1,0:T(8,128)(2,1)S(1)}, u32[]{:S(2)}, u32[]{:S(2)}) collective-permute-start(bf16[2048,128]{1,0:T(8,128)(2,1)S(1)} %gather_fusion.1), channel_id=1, source_target_pairs={{0,1},{1,2},{2,3},{3,4},{4,5},{5,6},{6,7},{8,9},{9,10},{10,11},{11... | collective-permute-start | bytes 1572872 | tf_op jit(solution)/shard_map/ppermute | solution.py:10
  88.1 7.3 %convert_element_type.20 = f32[24576,128]{1,0:T(8,128)} convert(bf16[24576,128]{1,0:T(8,128)(2,1)} %all-gather.2.cloned.1.call-done) | non-fusion elementwise | flops 3145728 | bytes 18874368 | tf_op jit(solution)/shard_map/convert_element_type | solution.py:30
  95.5 0.0 collective-permute-done
  95.5 19.5 %scatter_custom_fusion = f32[24576,128]{1,0:T(8,128)} fusion(f32[24576,128]{1,0:T(8,128)} %convert_element_type.20, s32[2048]{0:T(1024)S(1)} %bitcast.32, bf16[2048,128]{1,0:T(8,128)(2,1)S(1)} %collective-permute-done), kind=kCustom, calls=%fused_computation.14 | custom fusion | flops 524288 | bytes 13107200 | tf_op jit(solution)/shard_map/scatter-add | solution.py:31
  115.0 0.0 collective-permute-done.1
  115.0 19.5 %scatter_custom_fusion.1 = f32[24576,128]{1,0:T(8,128)} fusion(f32[24576,128]{1,0:T(8,128)} %scatter_custom_fusion, s32[2048]{0:T(1024)S(1)} %bitcast.30, bf16[2048,128]{1,0:T(8,128)(2,1)S(1)} %collective-permute-done.1), kind=kCustom, calls=%fused_computation.12 | custom fusion | flops 524288 | bytes 13107200 | tf_op jit(solution)/shard_map/scatter-add | solution.py:32
  134.5 10.8 %fusion.8 = f32[256,128]{0,1:T(8,128)} fusion(bf16[1,24576,256]{2,1,0:T(8,128)(2,1)} %param.9, f32[24576,128]{1,0:T(8,128)} %scatter_custom_fusion.1), kind=kOutput, calls=%fused_computation.11 | convolution fusion | flops 1613758464 | bytes 25296896 | tf_op jit(solution)/shard_map/dot_general | solution.py:37
  145.3 0.0 all-reduce.2.cloned.1.call-update
  145.3 69.8 %all-reduce.2.cloned.1.call-done = f32[256,128]{0,1:T(8,128)} async-done(((f32[256,128]{0,1:T(8,128)}), f32[256,128]{0,1:T(8,128)}) %all-reduce.2.cloned.1.call-update) | async-done | bytes 131088 | tf_op jit(solution)/shard_map/psum | solution.py:38
  215.1 0.9 constant_dynamic-slice_fusion
  216.1 0.7 copy.8
  (4 shorter events, 0.0 us)
Async XLA Ops:
  6.5 57.3 %all-gather.2.cloned.1.call-start = ((), (), s32[]{:S(2)}) async-start(), calls=%async_computation | async-start | bytes 7864320 | tf_op jit(solution)/shard_map/all_gather | solution.py:25
  7.9 6.7 %copy-start = (s32[1,2,2048]{2,1,0:T(2,128)S(1)}, s32[1,2,2048]{2,1,0:T(2,128)}, u32[]{:S(2)}) copy-start(s32[1,2,2048]{2,1,0:T(2,128)} %param.10) | copy-start | bytes 49156
  14.6 200.5 %all-reduce.2.cloned.1.call-start = ((), (), s32[]{:S(2)}) async-start(), calls=%async_computation.1 | async-start | bytes 262144 | tf_op jit(solution)/shard_map/psum | solution.py:38
  73.1 22.4 %collective-permute-start = (bf16[2048,128]{1,0:T(8,128)(2,1)S(1)}, bf16[2048,128]{1,0:T(8,128)(2,1)S(1)}, u32[]{:S(2)}, u32[]{:S(2)}) collective-permute-start(bf16[2048,128]{1,0:T(8,128)(2,1)S(1)} %gather_fusion), channel_id=1, source_target_pairs={{1,0},{2,1},{3,2},{4,3},{5,4},{6,5},{7,6},{9,8},{10,9},{11,10},{12... | collective-permute-start | bytes 1572872 | tf_op jit(solution)/shard_map/ppermute | solution.py:10
  83.6 31.4 %collective-permute-start.1 = (bf16[2048,128]{1,0:T(8,128)(2,1)S(1)}, bf16[2048,128]{1,0:T(8,128)(2,1)S(1)}, u32[]{:S(2)}, u32[]{:S(2)}) collective-permute-start(bf16[2048,128]{1,0:T(8,128)(2,1)S(1)} %gather_fusion.1), channel_id=1, source_target_pairs={{0,1},{1,2},{2,3},{3,4},{4,5},{5,6},{6,7},{8,9},{9,10},{10,11},{11... | collective-permute-start | bytes 1572872 | tf_op jit(solution)/shard_map/ppermute | solution.py:10
Sparse Core Ops, SparseCore 0:
  14.7 49.0 all-gather.1
  145.5 69.6 all-reduce.1
where the time goes:
time: 224 us
  waiting for transfers between devices  119 us (53%)
  other arithmetic  46.4 us (21%)
  local copies, waits for them, and re-layouts  20.7 us (9%)
  matrix products  17.5 us (8%)
  between operations  14.1 us (6%)
  starting transfers between devices  5.92 us (3%)
    psum x1, waiting for transfers between devices, shards(): full_gram = lax.psum(partial_gram, 'row')  69.8 us
    all_gather x1, waiting for transfers between devices, shards(): whole = lax.all_gather(local_rows, 'col', axis=0, tiled=True)  49.1 us
    scatter-add x1, other arithmetic, shards(): summed = summed.at[prev_rows].add(from_prev.astype(jnp.float32))  19.5 us
    scatter-add x1, other arithmetic, shards(): summed = summed.at[next_rows].add(from_next.astype(jnp.float32))  19.5 us
    dot_general x1, matrix products, shards(): lax.dot_general(columns, summed, contract, preferred_element_type=jnp.flo...  10.8 us
    gather x1, local copies, waits for them, and re-layouts, shards(): from_prev = passed_along(whole[next_rows], 'row', 1)  9.19 us
    gather x1, local copies, waits for them, and re-layouts, shards(): from_next = passed_along(whole[prev_rows], 'row', -1)  9.19 us
    convert_element_type x1, other arithmetic, shards(): summed = whole.astype(jnp.float32)  7.34 us
  transfers between devices with their start and end apart: 4, of which 2 were waited for; matrix products, arithmetic and copies ran while one was open for 16% of the time, Pallas kernels for 0%

commit v1 on v0

--- a/solution.py
+++ b/solution.py
@@ -1,13 +1,65 @@
+import functools
+
 import jax
 import jax.numpy as jnp
 from jax import lax
+from jax.experimental import pallas as pl
+from jax.experimental.pallas import tpu as pltpu
 from jax.sharding import PartitionSpec as P
+
+MESH = pl.DeviceIdType.MESH
 
 
 def passed_along(value, axis, steps):
     count = lax.axis_size(axis)
     leading, last = (max(0, -steps), min(count, count - steps))
     return lax.ppermute(value, axis, [(source, source + steps) for source in range(leading, last)])
+
+
+def scatter_sum_kernel(n, x_ref, out_ref, arrived, send_sem, recv_sem):
+    me = lax.axis_index("row")
+    column = lax.axis_index("col")
+    own = out_ref.shape[0]
+    barrier = pltpu.get_barrier_semaphore()
+    for step in range(1, n):
+        peer = lax.rem(me + step, n)
+        pl.semaphore_signal(barrier, inc=1, device_id=(column, peer), device_id_type=MESH)
+    pl.semaphore_wait(barrier, n - 1)
+    copies = []
+    for step in range(1, n):
+        peer = lax.rem(me + step, n)
+        copy = pltpu.make_async_remote_copy(
+            src_ref=x_ref.at[pl.ds(pl.multiple_of(peer * own, own), own)],
+            dst_ref=arrived.at[step - 1],
+            send_sem=send_sem.at[step - 1],
+            recv_sem=recv_sem.at[step - 1],
+            device_id=(column, peer),
+            device_id_type=MESH,
+        )
+        copy.start()
+        copies.append(copy)
+    total = x_ref[pl.ds(pl.multiple_of(me * own, own), own)]
+    for step, copy in enumerate(copies):
+        copy.wait()
+        total = total + arrived[step]
+    out_ref[...] = total
+
+
+def scatter_sum(x):
+    n = lax.axis_size("row")
+    own = x.shape[0] // n
+    return pl.pallas_call(
+        functools.partial(scatter_sum_kernel, n),
+        out_shape=jax.ShapeDtypeStruct((own, x.shape[1]), jnp.float32),
+        in_specs=[pl.BlockSpec(memory_space=pltpu.VMEM)],
+        out_specs=pl.BlockSpec(memory_space=pltpu.VMEM),
+        scratch_shapes=[
+            pltpu.VMEM((n - 1, own, x.shape[1]), jnp.float32),
+            pltpu.SemaphoreType.DMA((n - 1,)),
+            pltpu.SemaphoreType.DMA((n - 1,)),
+        ],
+        compiler_params=pltpu.CompilerParams(collective_id=0, has_side_effects=True),
+    )(x)
 
 
 def shards(panel, stiffness, mass, resident, face_rows, counts):
@@ -25,19 +77,16 @@
     whole = lax.all_gather(local_rows, "col", axis=0, tiled=True)
     prev_rows = face_rows[0, 0]
     next_rows = face_rows[0, 1]
+    columns = resident[0]
+    at_next = columns[next_rows]
+    at_prev = columns[prev_rows]
     from_next = passed_along(whole[prev_rows], "row", -1)
     from_prev = passed_along(whole[next_rows], "row", 1)
-    summed = whole.astype(jnp.float32)
-    summed = summed.at[next_rows].add(from_next.astype(jnp.float32))
-    summed = summed.at[prev_rows].add(from_prev.astype(jnp.float32))
-    summed = summed.astype(jnp.bfloat16)
-    columns = resident[0]
     contract = (((0,), (0,)), ((), ()))
-    own_rows = columns.shape[1] // lax.axis_size("row")
-    partial_gram = lax.dot_general(columns, summed, contract, preferred_element_type=jnp.float32)
-    full_gram = lax.psum(partial_gram, "row")
-    gram = lax.dynamic_slice_in_dim(full_gram, lax.axis_index("row") * own_rows, own_rows, 0)
-    return gram
+    partial_gram = lax.dot_general(columns, whole, contract, preferred_element_type=jnp.float32)
+    partial_gram += lax.dot_general(at_next, from_next, contract, preferred_element_type=jnp.float32)
+    partial_gram += lax.dot_general(at_prev, from_prev, contract, preferred_element_type=jnp.float32)
+    return scatter_sum(partial_gram)
 
 
 def solution(mesh):

time: 224 us -> 120 us (0.54)
  waiting for transfers between devices: 119 us -> 27.5 us
  other arithmetic: 46.4 us -> 0.04 us
  local copies, waits for them, and re-layouts: 20.7 us -> 46.4 us
  Pallas kernels: 0 us -> 8.24 us
    psum x1 -> x0, waiting for transfers between devices: 69.8 us -> none  [shards(): full_gram = lax.psum(partial_gram, 'row')]
    scatter-add x2 -> x0, other arithmetic: 39 us -> none  [the longest x1 19.5 us: shards(): summed = summed.at[prev_rows].add(from_prev.astype(jnp.float32))]
    gather x0 -> x2, local copies, waits for them, and re-layouts: none -> 25.9 us  [the longest x1 13.1 us: shards(): at_next = columns[next_rows]]
    all_gather x1, waiting for transfers between devices: 49.1 us -> 23.2 us  [shards(): whole = lax.all_gather(local_rows, 'col', axis=0, tiled=True)]
    pallas_call x0 -> x1, Pallas kernels: none -> 8.24 us  [scatter_sum(): pl.pallas_call(functools.partial(scatter_sum_kernel, n), out_shape=jax.Sh...]
    convert_element_type x1 -> x0, other arithmetic: 7.34 us -> none  [shards(): summed = whole.astype(jnp.float32)]
    ppermute x2, waiting for transfers between devices: 0.01 us -> 4.28 us  [passed_along(): lax.ppermute(value, axis, [(source, source + steps) for source in range(l...]
    dot_general x1 -> x3, matrix products: 10.8 us -> 11.2 us  [the longest x1 8.59 us: shards(): lax.dot_general(columns, whole, contract, preferred_element_type=jnp.floa...]
  transfers between devices with their start and end apart: 4 -> 3, of which waited for: 2 -> 2; matrix products, arithmetic and copies ran while one was open for 16% -> 38% of each run, Pallas kernels for 0% -> 0%
where the time goes in v1:
time: 120 us
  local copies, waits for them, and re-layouts  46.4 us (39%)
  waiting for transfers between devices  27.5 us (23%)
  matrix products  17.9 us (15%)
  between operations  14.2 us (12%)
  Pallas kernels  8.24 us (7%)
  starting transfers between devices  5.49 us (5%)
    all_gather x1, waiting for transfers between devices, shards(): whole = lax.all_gather(local_rows, 'col', axis=0, tiled=True)  23.2 us
    gather x1, local copies, waits for them, and re-layouts, shards(): at_next = columns[next_rows]  13.1 us
    gather x1, local copies, waits for them, and re-layouts, shards(): at_prev = columns[prev_rows]  12.8 us
    gather x1, local copies, waits for them, and re-layouts, shards(): from_prev = passed_along(whole[next_rows], 'row', 1)  9.19 us
    gather x1, local copies, waits for them, and re-layouts, shards(): from_next = passed_along(whole[prev_rows], 'row', -1)  9.19 us
    dot_general x1, matrix products, shards(): lax.dot_general(columns, whole, contract, preferred_element_type=jnp.floa...  8.59 us
    pallas_call x1, Pallas kernels, scatter_sum(): pl.pallas_call(functools.partial(scatter_sum_kernel, n), out_shape=jax.Sh...  8.24 us
    dot_general x1, matrix products, shards(): jnp.einsum('enm,ems->ens', stiffness[0], values, preferred_element_type=j...  6.64 us
  transfers between devices with their start and end apart: 3, of which 2 were waited for; matrix products, arithmetic and copies ran while one was open for 38% of the time, Pallas kernels for 0%

profile of v1, /device:TPU:0, one launch (start us, length us, event | category | flops | bytes accessed | tf_op | source)
XLA Modules:
  0.0 119.7 jit_solution(1570282417955512798)
XLA Ops:
  6.5 0.0 all-gather.2.cloned.1.call-start
  6.5 0.7 copy.12
  7.9 0.0 copy-start
  8.0 6.6 %select_convert_fusion = bf16[12,512,128]{2,1,0:T(8,128)(2,1)} fusion(bf16[1,12,512,512]{3,2,1,0:T(8,128)(2,1)} %param.7, bf16[1,12,512,128]{3,2,1,0:T(8,128)(2,1)} %param.6, f32[12,512]{1,0:T(8,128)S(1)} %bitcast.33, pred[12]{0:T(512)(128)(4,1)S(1)} %add_compare_fusion), kind=kOutput, calls=%fused_computation.6 | convolution fusion | flops 809238528 | bytes 9461772 | tf_op jit(solution)/shard_map/enm,ems->ens/dot_general | solution.py:73
  14.6 0.0 all-gather.2.cloned.1.call-update
  14.6 0.0 copy-done
  14.7 12.8 %gather_fusion.2 = bf16[2048,256]{1,0:T(8,128)(2,1)S(1)} fusion(bf16[24576,256]{1,0:T(8,128)(2,1)} %bitcast.30, s32[2048]{0:T(1024)S(1)} %broadcast_clamp_fusion), kind=kCustom, calls=%fused_computation.2 | custom fusion | bytes 2105344 | tf_op jit(solution)/shard_map/gather | solution.py:82
  27.5 13.1 %gather_fusion = bf16[2048,256]{1,0:T(8,128)(2,1)S(1)} fusion(bf16[24576,256]{1,0:T(8,128)(2,1)} %bitcast.31, s32[2048]{0:T(1024)S(1)} %broadcast_clamp_fusion.1), kind=kCustom, calls=%fused_computation | custom fusion | bytes 2105344 | tf_op jit(solution)/shard_map/gather | solution.py:81
  40.6 23.2 %all-gather.2.cloned.1.call-done = bf16[24576,128]{1,0:T(8,128)(2,1)} async-done(((bf16[6144,128]{1,0:T(8,128)(2,1)}), bf16[24576,128]{1,0:T(8,128)(2,1)}) %all-gather.2.cloned.1.call-update) | async-done | bytes 6291472 | tf_op jit(solution)/shard_map/all_gather | solution.py:77
  63.9 9.2 %gather_fusion.3 = bf16[2048,128]{1,0:T(8,128)(2,1)S(1)} fusion(bf16[24576,128]{1,0:T(8,128)(2,1)} %all-gather.2.cloned.1.call-done, s32[2048]{0:T(1024)S(1)} %broadcast_clamp_fusion.1), kind=kCustom, calls=%fused_computation.3 | custom fusion | bytes 1056768 | tf_op jit(solution)/shard_map/gather | solution.py:84
  73.1 4.2 %collective-permute-start.1 = (bf16[2048,128]{1,0:T(8,128)(2,1)S(1)}, bf16[2048,128]{1,0:T(8,128)(2,1)}, u32[]{:S(2)}, u32[]{:S(2)}) collective-permute-start(bf16[2048,128]{1,0:T(8,128)(2,1)S(1)} %gather_fusion.3), channel_id=1, source_target_pairs={{0,1},{1,2},{2,3},{3,4},{4,5},{5,6},{6,7},{8,9},{9,10},{10,11},{11... | collective-permute-start | bytes 1572872 | tf_op jit(solution)/shard_map/ppermute | solution.py:16
  77.3 9.2 %gather_fusion.1 = bf16[2048,128]{1,0:T(8,128)(2,1)S(1)} fusion(bf16[24576,128]{1,0:T(8,128)(2,1)} %all-gather.2.cloned.1.call-done, s32[2048]{0:T(1024)S(1)} %broadcast_clamp_fusion), kind=kCustom, calls=%fused_computation.1 | custom fusion | bytes 1056768 | tf_op jit(solution)/shard_map/gather | solution.py:83
  86.4 1.3 %collective-permute-start = (bf16[2048,128]{1,0:T(8,128)(2,1)S(1)}, bf16[2048,128]{1,0:T(8,128)(2,1)S(1)}, u32[]{:S(2)}, u32[]{:S(2)}) collective-permute-start(bf16[2048,128]{1,0:T(8,128)(2,1)S(1)} %gather_fusion.1), channel_id=1, source_target_pairs={{1,0},{2,1},{3,2},{4,3},{5,4},{6,5},{7,6},{9,8},{10,9},{11,10},{12... | collective-permute-start | bytes 1572872 | tf_op jit(solution)/shard_map/ppermute | solution.py:16
  87.7 8.6 %convolution_bitcast_fusion = f32[256,128]{1,0:T(8,128)S(1)} fusion(bf16[24576,128]{1,0:T(8,128)(2,1)} %all-gather.2.cloned.1.call-done, bf16[1,24576,256]{2,1,0:T(8,128)(2,1)} %param.9), kind=kOutput, calls=%fused_computation.10 | convolution fusion | flops 1610612736 | bytes 19005440 | tf_op jit(solution)/shard_map/dot_general | solution.py:86
  96.3 0.0 collective-permute-done.1
  96.4 1.5 %fusion.7 = f32[256,128]{1,0:T(8,128)S(1)} fusion(bf16[2048,256]{1,0:T(8,128)(2,1)S(1)} %gather_fusion.2, bf16[2048,128]{1,0:T(8,128)(2,1)} %collective-permute-done.1), kind=kOutput, calls=%fused_computation.18 | convolution fusion | flops 134217728 | bytes 1703936 | tf_op jit(solution)/shard_map/dot_general | solution.py:88
  97.9 4.3 %collective-permute-done = bf16[2048,128]{1,0:T(8,128)(2,1)S(1)} collective-permute-done((bf16[2048,128]{1,0:T(8,128)(2,1)S(1)}, bf16[2048,128]{1,0:T(8,128)(2,1)S(1)}, u32[]{:S(2)}, u32[]{:S(2)}) %collective-permute-start) | collective-permute-done | bytes 524320 | tf_op jit(solution)/shard_map/ppermute | solution.py:16
  102.1 1.1 fusion.5.x_ref
  103.3 8.2 %shard_map.64 = f32[32,128]{1,0:T(8,128)} custom-call(f32[256,128]{1,0:T(8,128)} %fusion.5.x_ref), custom_call_target="tpu_custom_call" | custom-call | tf_op jit(solution)/shard_map/pallas_call | solution.py:51
  111.5 1.3 %copy.15 = f32[32,128]{1,0:T(8,128)} copy(f32[32,128]{1,0:T(8,128)} %shard_map.64) | data formatting | bytes 32768
  (4 shorter events, 0.0 us)
Async XLA Ops:
  6.5 57.3 %all-gather.2.cloned.1.call-start = ((), (), s32[]{:S(2)}) async-start(), calls=%async_computation | async-start | bytes 7864320 | tf_op jit(solution)/shard_map/all_gather | solution.py:77
  7.9 6.7 %copy-start = (s32[1,2,2048]{2,1,0:T(2,128)S(1)}, s32[1,2,2048]{2,1,0:T(2,128)}, u32[]{:S(2)}) copy-start(s32[1,2,2048]{2,1,0:T(2,128)} %param.10) | copy-start | bytes 49156
  73.1 23.3 %collective-permute-start.1 = (bf16[2048,128]{1,0:T(8,128)(2,1)S(1)}, bf16[2048,128]{1,0:T(8,128)(2,1)}, u32[]{:S(2)}, u32[]{:S(2)}) collective-permute-start(bf16[2048,128]{1,0:T(8,128)(2,1)S(1)} %gather_fusion.3), channel_id=1, source_target_pairs={{0,1},{1,2},{2,3},{3,4},{4,5},{5,6},{6,7},{8,9},{9,10},{10,11},{11... | collective-permute-start | bytes 1572872 | tf_op jit(solution)/shard_map/ppermute | solution.py:16
  86.4 15.7 %collective-permute-start = (bf16[2048,128]{1,0:T(8,128)(2,1)S(1)}, bf16[2048,128]{1,0:T(8,128)(2,1)S(1)}, u32[]{:S(2)}, u32[]{:S(2)}) collective-permute-start(bf16[2048,128]{1,0:T(8,128)(2,1)S(1)} %gather_fusion.1), channel_id=1, source_target_pairs={{1,0},{2,1},{3,2},{4,3},{5,4},{6,5},{7,6},{9,8},{10,9},{11,10},{12... | collective-permute-start | bytes 1572872 | tf_op jit(solution)/shard_map/ppermute | solution.py:16
Sparse Core Ops, SparseCore 0:
  14.7 49.0 all-gather.1

commit v2 on v0

v2 whole, which is shorter than its diff:
```python
import functools

import jax
import jax.numpy as jnp
from jax import lax
from jax.experimental import pallas as pl
from jax.experimental.pallas import tpu as pltpu
from jax.sharding import PartitionSpec as P

MESH = pl.DeviceIdType.MESH
ROWS_FIRST = (((0,), (0,)), ((), ()))
DEPTH = 4
GATHER_PIECES = 8
GROUP = 8


def gram_kernel(
    n, panel, mass, counts, faces, stiffness, resident, out,
    applied, res, wide, kbuf, rbuf, res_rows, picked, leaving, arrived, acc, gram, terms,
    k_sem, r_sem, far_send, far_recv, mate_send, mate_recv, on_send, on_recv,
    face_send, face_recv, ffar_send, ffar_recv, fmate_send, fmate_recv, fon_send, fon_recv,
    sum_send, sum_recv,
):
    me = lax.axis_index("row")
    c = lax.axis_index("col")
    mate = (c // 2) * 2 + (1 - c % 2)
    far = (1 - c // 2) * 2 + c % 2
    opposite = (1 - c // 2) * 2 + (1 - c % 2)
    slots, nodes = panel.shape[1], panel.shape[2]
    face_n = faces.shape[2]
    quarter = face_n // 4
    own = out.shape[0]
    all_slots = applied.shape[0]

    def stiff_copy(e):
        return pltpu.make_async_copy(stiffness.at[0, e], kbuf.at[e % DEPTH], k_sem.at[e % DEPTH])

    def res_copy(s):
        rows = pl.ds(pl.multiple_of(s * nodes, nodes), nodes)
        return pltpu.make_async_copy(resident.at[0, rows], rbuf.at[s % DEPTH], r_sem.at[s % DEPTH])

    def to(buffer, index, send, recv, k, column):
        return pltpu.make_async_remote_copy(
            src_ref=buffer.at[index], dst_ref=buffer.at[index], send_sem=send.at[k], recv_sem=recv.at[k],
            device_id=(column, me), device_id_type=MESH)

    for e in range(DEPTH):
        stiff_copy(e).start()
    for s in range(DEPTH):
        res_copy(s).start()
    barrier = pltpu.get_barrier_semaphore()
    for step in range(1, n):
        pl.semaphore_signal(barrier, inc=1, device_id=(c, lax.rem(me + step, n)), device_id_type=MESH)
    for column in (mate, far):
        pl.semaphore_signal(barrier, inc=1, device_id=(column, me), device_id_type=MESH)
    pl.semaphore_wait(barrier, n + 1)

    acc[...] = jnp.zeros_like(acc)
    node_ids = lax.broadcasted_iota(jnp.int32, (nodes, mass.shape[1]), 1)

    def apply_slot(e, carry):
        stiff_copy(e).wait()
        values = panel[0, e]
        product = jnp.dot(kbuf[e % DEPTH], values, preferred_element_type=jnp.float32)
        weight = jnp.sum(jnp.where(node_ids == e, mass[...], 0.0), axis=1, keepdims=True)
        product = product + weight * values.astype(jnp.float32)
        live = jnp.where(c * slots + e < counts[0], 1.0, 0.0)
        applied[c * slots + e] = (product * live).astype(jnp.bfloat16)
        to(applied, c * slots + e, far_send, far_recv, e, far).start()
        to(applied, c * slots + e, mate_send, mate_recv, e, mate).start()

        @pl.when(e + DEPTH < slots)
        def _():
            stiff_copy(e + DEPTH).start()
        return carry

    lax.fori_loop(0, slots, apply_slot, 0)

    def widen_resident(s, carry):
        res_copy(s).wait()
        res[pl.ds(pl.multiple_of(s * nodes, nodes), nodes), :] = rbuf[s % DEPTH].astype(jnp.float32)

        @pl.when(s + DEPTH < all_slots)
        def _():
            res_copy(s + DEPTH).start()
        return carry

    lax.fori_loop(0, all_slots, widen_resident, 0)

    def add_slot(slot):
        rows = pl.ds(pl.multiple_of(slot * nodes, nodes), nodes)
        block = applied[slot]
        wide[rows, :] = block.astype(jnp.float32)
        acc[...] += lax.dot_general(
            block, res[rows, :].astype(jnp.bfloat16), ROWS_FIRST, preferred_element_type=jnp.float32)

    piece_groups = 2 * face_n // GROUP // GATHER_PIECES

    def gather_resident(piece):
        def group(i, carry):
            g = piece * piece_groups + i
            for t in range(GROUP):
                j = g * GROUP + t
                row = faces[0, j // face_n, j % face_n]
                res_rows[g, t:t + 1, :] = res[pl.ds(row, 1), :]
            return carry
        lax.fori_loop(0, piece_groups, group, 0)

    def exchange_slot(e, carry):
        add_slot(c * slots + e)
        to(applied, mate * slots + e, mate_send, mate_recv, e, mate).wait_recv()
        add_slot(mate * slots + e)

        @pl.when(e < GATHER_PIECES)
        def _():
            gather_resident(e)

        to(applied, far * slots + e, far_send, far_recv, e, far).wait_recv()
        to(applied, far * slots + e, on_send, on_recv, e, mate).start()
        add_slot(far * slots + e)

        @pl.when(e > 0)
        def _():
            to(applied, opposite * slots + e - 1, on_send, on_recv, e - 1, mate).wait_recv()
            add_slot(opposite * slots + e - 1)
        return carry

    lax.fori_loop(0, slots, exchange_slot, 0)
    to(applied, opposite * slots + slots - 1, on_send, on_recv, slots - 1, mate).wait_recv()
    add_slot(opposite * slots + slots - 1)

    has = (me < n - 1, me > 0)
    target = (jnp.maximum(me - 1, 0), jnp.minimum(me + 1, n - 1))
    sends = (me > 0, me < n - 1)

    def face_copy(l):
        return pltpu.make_async_remote_copy(
            src_ref=leaving.at[l], dst_ref=arrived.at[l, c], send_sem=face_send.at[l], recv_sem=face_recv.at[l],
            device_id=(c, target[l]), device_id_type=MESH)

    for l in range(2):
        def group(i, carry, l=l):
            for t in range(GROUP):
                row = faces[0, l, c * quarter + i * GROUP + t]
                picked[i, t:t + 1, :] = wide[pl.ds(row, 1), :]
            return carry
        lax.fori_loop(0, quarter // GROUP, group, 0)
        leaving[l] = picked[...].reshape(quarter, picked.shape[2]).astype(jnp.bfloat16)

        @pl.when(sends[l])
        def _(l=l):
            face_copy(l).start()

    def share(l, column, send, recv, to_column):
        return pltpu.make_async_remote_copy(
            src_ref=arrived.at[l, column], dst_ref=arrived.at[l, column], send_sem=send.at[l], recv_sem=recv.at[l],
            device_id=(to_column, me), device_id_type=MESH)

    def add_face(l, column):
        groups = quarter // GROUP
        start = (1 - l) * (face_n // GROUP) + column * groups
        rows = res_rows[pl.ds(start, groups)].reshape(quarter, res_rows.shape[2])
        acc[...] += lax.dot_general(
            arrived[l, column], rows.astype(jnp.bfloat16), ROWS_FIRST, preferred_element_type=jnp.float32)

    for l in range(2):
        @pl.when(has[l])
        def _(l=l):
            face_copy(l).wait_recv()

        @pl.when(jnp.logical_not(has[l]))
        def _(l=l):
            arrived[l, c] = jnp.zeros(arrived.shape[2:], jnp.bfloat16)

        share(l, c, ffar_send, ffar_recv, far).start()
        share(l, c, fmate_send, fmate_recv, mate).start()
    for l in range(2):
        add_face(l, c)
        share(l, mate, fmate_send, fmate_recv, mate).wait_recv()
        add_face(l, mate)
    for l in range(2):
        share(l, far, ffar_send, ffar_recv, far).wait_recv()
        share(l, far, fon_send, fon_recv, mate).start()
        add_face(l, far)
    for l in range(2):
        share(l, opposite, fon_send, fon_recv, mate).wait_recv()
        add_face(l, opposite)

    gram[...] = acc[...].T
    copies = []
    for step in range(1, n):
        peer = lax.rem(me + step, n)
        copy = pltpu.make_async_remote_copy(
            src_ref=gram.at[pl.ds(pl.multiple_of(peer * own, own), own)], dst_ref=terms.at[step - 1],
            send_sem=sum_send.at[step - 1], recv_sem=sum_recv.at[step - 1],
            device_id=(c, peer), device_id_type=MESH)
        copy.start()
        copies.append(copy)

    def drain(e, carry):
        to(applied, c * slots + e, far_send, far_recv, e, far).wait_send()
        to(applied, c * slots + e, mate_send, mate_recv, e, mate).wait_send()
        to(applied, far * slots + e, on_send, on_recv, e, mate).wait_send()
        return carry

    lax.fori_loop(0, slots, drain, 0)
    for l in range(2):
        @pl.when(sends[l])
        def _(l=l):
            face_copy(l).wait_send()
        share(l, c, ffar_send, ffar_recv, far).wait_send()
        share(l, c, fmate_send, fmate_recv, mate).wait_send()
        share(l, far, fon_send, fon_recv, mate).wait_send()
    total = gram[pl.ds(pl.multiple_of(me * own, own), own), :]
    for step, copy in enumerate(copies):
        copy.wait_recv()
        total = total + terms[step]
    for copy in copies:
        copy.wait_send()
    out[...] = total


def shards(panel, stiffness, mass, resident, face_rows, counts):
    n = lax.axis_size("row")
    columns = lax.axis_size("col")
    slots, nodes, width = panel.shape[1:]
    rows, kept = resident.shape[1:]
    face_n = face_rows.shape[2]
    quarter = face_n // columns
    own = kept // n
    bf16, f32 = jnp.bfloat16, jnp.float32
    dma = pltpu.SemaphoreType.DMA
    vmem = pl.BlockSpec(memory_space=pltpu.VMEM)
    smem = pl.BlockSpec(memory_space=pltpu.SMEM)
    anywhere = pl.BlockSpec(memory_space=pl.ANY)
    flops = 2 * slots * nodes * nodes * width + 2 * (rows + 2 * face_n) * kept * width
    return pl.pallas_call(
        functools.partial(gram_kernel, n),
        out_shape=jax.ShapeDtypeStruct((own, width), f32),
        in_specs=[vmem, vmem, smem, smem, anywhere, anywhere],
        out_specs=vmem,
        scratch_shapes=[
            pltpu.VMEM((columns * slots, nodes, width), bf16),
            pltpu.VMEM((rows, kept), f32),
            pltpu.VMEM((rows, width), f32),
            pltpu.VMEM((DEPTH, nodes, nodes), bf16),
            pltpu.VMEM((DEPTH, nodes, kept), bf16),
            pltpu.VMEM((2 * face_n // GROUP, GROUP, kept), f32),
            pltpu.VMEM((quarter // GROUP, GROUP, width), f32),
            pltpu.VMEM((2, quarter, width), bf16),
            pltpu.VMEM((2, columns, quarter, width), bf16),
            pltpu.VMEM((width, kept), f32),
            pltpu.VMEM((kept, width), f32),
            pltpu.VMEM((n - 1, own, width), f32),
            dma((DEPTH,)), dma((DEPTH,)),
            dma((slots,)), dma((slots,)), dma((slots,)), dma((slots,)), dma((slots,)), dma((slots,)),
            dma((2,)), dma((2,)), dma((2,)), dma((2,)), dma((2,)), dma((2,)), dma((2,)), dma((2,)),
            dma((n - 1,)), dma((n - 1,)),
        ],
        compiler_params=pltpu.CompilerParams(
            collective_id=0, has_side_effects=True, vmem_limit_bytes=62 * 1024 * 1024),
        cost_estimate=pl.CostEstimate(
            flops=flops, bytes_accessed=2 * (slots * nodes * (nodes + width) + rows * kept), transcendentals=0),
    )(panel, mass[0].T, counts, face_rows, stiffness, resident)


def solution(mesh):
    in_specs = (
        P("row", "col", None, None),
        P("row", "col", None, None),
        P("row", "col", None),
        P("row", None, "col"),
        P("row", None, None),
        P("row"),
    )
    out_specs = P(("col", "row"), None)
    return jax.shard_map(shards, mesh=mesh, in_specs=in_specs, out_specs=out_specs, check_vma=False)
```

time: 224 us -> 102 us (0.46)
  waiting for transfers between devices: 119 us -> 0 us
  Pallas kernels: 0 us -> 97.5 us
  other arithmetic: 46.4 us -> 0 us
  local copies, waits for them, and re-layouts: 20.7 us -> 2.9 us
  matrix products: 17.5 us -> 0 us
  between operations: 14.1 us -> 0.66 us
  starting transfers between devices: 5.92 us -> 0 us
    pallas_call x0 -> x1, Pallas kernels: none -> 97.5 us  [shards(): pl.pallas_call(functools.partial(gram_kernel, n), out_shape=jax.ShapeDtyp...]
    psum x1 -> x0, waiting for transfers between devices: 69.8 us -> none  [shards(): full_gram = lax.psum(partial_gram, 'row')]
    all_gather x1 -> x0, waiting for transfers between devices: 49.1 us -> none  [shards(): whole = lax.all_gather(local_rows, 'col', axis=0, tiled=True)]
    scatter-add x2 -> x0, other arithmetic: 39 us -> none  [the longest x1 19.5 us: shards(): summed = summed.at[prev_rows].add(from_prev.astype(jnp.float32))]
    gather x2 -> x0, local copies, waits for them, and re-layouts: 18.4 us -> none  [the longest x1 9.19 us: shards(): from_prev = passed_along(whole[next_rows], 'row', 1)]
    dot_general x2 -> x0, matrix products: 17.5 us -> none  [the longest x1 10.8 us: shards(): lax.dot_general(columns, summed, contract, preferred_element_type=jnp.flo...]
    convert_element_type x1 -> x0, other arithmetic: 7.34 us -> none  [shards(): summed = whole.astype(jnp.float32)]
    ppermute x2 -> x0, starting transfers between devices: 5.87 us -> none  [passed_along(): lax.ppermute(value, axis, [(source, source + steps) for source in range(l...]
  transfers between devices with their start and end apart: 4 -> 0, of which waited for: 2 -> 0; matrix products, arithmetic and copies ran while one was open for 16% -> 0% of each run, Pallas kernels for 0% -> 0%
where the time goes in v2:
time: 102 us; the launch traced here: 101 us
  Pallas kernels  97.5 us (96%)
  local copies, waits for them, and re-layouts  2.9 us (3%)
    pallas_call x1, Pallas kernels, shards(): pl.pallas_call(functools.partial(gram_kernel, n), out_shape=jax.ShapeDtyp...  97.5 us
    unnamed x2, local copies, waits for them, and re-layouts  2.9 us

profile of v2, /device:TPU:0, one launch (start us, length us, event | category | flops | bytes accessed | tf_op | source)
XLA Modules:
  0.0 101.1 jit_solution(2521865995724752824)
XLA Ops:
  0.7 1.6 %copy.7 = f32[1,12,512]{1,2,0:T(8,128)} copy(f32[1,12,512]{2,0,1:T(1,128)} %param.8) | data formatting | bytes 49152 | tf_op args[2]
  2.2 97.5 %shard_map.64 = f32[32,128]{1,0:T(8,128)} custom-call(bf16[1,12,512,128]{3,2,1,0:T(8,128)(2,1)} %panel.1, f32[512,12]{1,0:T(8,128)} %bitcast.3, s32[1]{0:T(128)S(6)} %copy.9.counts, s32[1,2,2048]{2,1,0:T(2,128)} %faces.1, bf16[1,12,512,512]{3,2,1,0:T(8,128)(2,1)} %stiffness.1, bf16[1,24576,256]{2,1,0:T(8,128)(2,1)} %resident.1), custom_call_target="tpu_custom_call" | custom-call | flops 2684354560 | bytes 20447232 | tf_op jit(solution)/shard_map/pallas_call | solution.py:237
  99.7 1.3 %copy.10 = f32[32,128]{1,0:T(8,128)} copy(f32[32,128]{1,0:T(8,128)} %shard_map.64) | data formatting | bytes 32768

commit v3 on v2

--- a/solution.py
+++ b/solution.py
@@ -12,6 +12,7 @@
 DEPTH = 4
 GATHER_PIECES = 8
 GROUP = 8
+BATCH = 16
 
 
 def gram_kernel(
@@ -33,11 +34,11 @@
     all_slots = applied.shape[0]
 
     def stiff_copy(e):
-        return pltpu.make_async_copy(stiffness.at[0, e], kbuf.at[e % DEPTH], k_sem.at[e % DEPTH])
+        return pltpu.make_async_copy(stiffness.at[0, e], kbuf.at[lax.rem(e, DEPTH)], k_sem.at[lax.rem(e, DEPTH)])
 
     def res_copy(s):
         rows = pl.ds(pl.multiple_of(s * nodes, nodes), nodes)
-        return pltpu.make_async_copy(resident.at[0, rows], rbuf.at[s % DEPTH], r_sem.at[s % DEPTH])
+        return pltpu.make_async_copy(resident.at[0, rows], rbuf.at[lax.rem(s, DEPTH)], r_sem.at[lax.rem(s, DEPTH)])
 
     def to(buffer, index, send, recv, k, column):
         return pltpu.make_async_remote_copy(
@@ -45,9 +46,9 @@
             device_id=(column, me), device_id_type=MESH)
 
     for e in range(DEPTH):
-        stiff_copy(e).start()
+        stiff_copy(jnp.int32(e)).start()
     for s in range(DEPTH):
-        res_copy(s).start()
+        res_copy(jnp.int32(s)).start()
     barrier = pltpu.get_barrier_semaphore()
     for step in range(1, n):
         pl.semaphore_signal(barrier, inc=1, device_id=(c, lax.rem(me + step, n)), device_id_type=MESH)
@@ -56,14 +57,17 @@
     pl.semaphore_wait(barrier, n + 1)
 
     acc[...] = jnp.zeros_like(acc)
-    node_ids = lax.broadcasted_iota(jnp.int32, (nodes, mass.shape[1]), 1)
+
+    def node_weights(e):
+        width = panel.shape[3]
+        pieces = [jnp.broadcast_to(mass[e, :, k:k + width], (width, width)).T for k in range(0, nodes, width)]
+        return jnp.concatenate(pieces, axis=0)
 
     def apply_slot(e, carry):
         stiff_copy(e).wait()
         values = panel[0, e]
-        product = jnp.dot(kbuf[e % DEPTH], values, preferred_element_type=jnp.float32)
-        weight = jnp.sum(jnp.where(node_ids == e, mass[...], 0.0), axis=1, keepdims=True)
-        product = product + weight * values.astype(jnp.float32)
+        product = jnp.dot(kbuf[lax.rem(e, DEPTH)], values, preferred_element_type=jnp.float32)
+        product = product + node_weights(e) * values.astype(jnp.float32)
         live = jnp.where(c * slots + e < counts[0], 1.0, 0.0)
         applied[c * slots + e] = (product * live).astype(jnp.bfloat16)
         to(applied, c * slots + e, far_send, far_recv, e, far).start()
@@ -78,7 +82,7 @@
 
     def widen_resident(s, carry):
         res_copy(s).wait()
-        res[pl.ds(pl.multiple_of(s * nodes, nodes), nodes), :] = rbuf[s % DEPTH].astype(jnp.float32)
+        res[pl.ds(pl.multiple_of(s * nodes, nodes), nodes), :] = rbuf[lax.rem(s, DEPTH)].astype(jnp.float32)
 
         @pl.when(s + DEPTH < all_slots)
         def _():
@@ -94,17 +98,22 @@
         acc[...] += lax.dot_general(
             block, res[rows, :].astype(jnp.bfloat16), ROWS_FIRST, preferred_element_type=jnp.float32)
 
-    piece_groups = 2 * face_n // GROUP // GATHER_PIECES
+    def gather_rows(source, l, first, target, target_first, count):
+        def groups(i, carry):
+            base = pl.multiple_of(first + i * BATCH, BATCH)
+            rows = [faces[0, l, base + t] for t in range(BATCH)]
+            values = [source[pl.ds(row, 1), :] for row in rows]
+            for t, value in enumerate(values):
+                target[target_first + i * (BATCH // GROUP) + t // GROUP, t % GROUP:t % GROUP + 1, :] = value
+            return carry
+        lax.fori_loop(0, count // BATCH, groups, 0)
+
+    piece_rows = 2 * face_n // GATHER_PIECES
+    half = GATHER_PIECES // 2
 
     def gather_resident(piece):
-        def group(i, carry):
-            g = piece * piece_groups + i
-            for t in range(GROUP):
-                j = g * GROUP + t
-                row = faces[0, j // face_n, j % face_n]
-                res_rows[g, t:t + 1, :] = res[pl.ds(row, 1), :]
-            return carry
-        lax.fori_loop(0, piece_groups, group, 0)
+        gather_rows(res, lax.div(piece, half), lax.rem(piece, half) * piece_rows,
+                    res_rows, piece * (piece_rows // GROUP), piece_rows)
 
     def exchange_slot(e, carry):
         add_slot(c * slots + e)
@@ -139,12 +148,7 @@
             device_id=(c, target[l]), device_id_type=MESH)
 
     for l in range(2):
-        def group(i, carry, l=l):
-            for t in range(GROUP):
-                row = faces[0, l, c * quarter + i * GROUP + t]
-                picked[i, t:t + 1, :] = wide[pl.ds(row, 1), :]
-            return carry
-        lax.fori_loop(0, quarter // GROUP, group, 0)
+        gather_rows(wide, l, c * quarter, picked, 0, quarter)
         leaving[l] = picked[...].reshape(quarter, picked.shape[2]).astype(jnp.bfloat16)
 
         @pl.when(sends[l])
@@ -261,7 +265,7 @@
             collective_id=0, has_side_effects=True, vmem_limit_bytes=62 * 1024 * 1024),
         cost_estimate=pl.CostEstimate(
             flops=flops, bytes_accessed=2 * (slots * nodes * (nodes + width) + rows * kept), transcendentals=0),
-    )(panel, mass[0].T, counts, face_rows, stiffness, resident)
+    )(panel, mass.transpose(1, 0, 2), counts, face_rows, stiffness, resident)
 
 
 def solution(mesh):

time: 102 us -> 73.8 us (0.72)
  Pallas kernels: 97.5 us -> 71.2 us
  local copies, waits for them, and re-layouts: 2.9 us -> 1.32 us
    pallas_call x1, Pallas kernels: 97.5 us -> 71.2 us  [shards(): pl.pallas_call(functools.partial(gram_kernel, n), out_shape=jax.ShapeDtyp...]
    unnamed x2 -> x1, local copies, waits for them, and re-layouts: 2.9 us -> 1.32 us
where the time goes in v3:
time: 73.8 us; the launch traced here: 73.2 us
  Pallas kernels  71.2 us (96%)
  local copies, waits for them, and re-layouts  1.32 us (2%)
    pallas_call x1, Pallas kernels, shards(): pl.pallas_call(functools.partial(gram_kernel, n), out_shape=jax.ShapeDtyp...  71.2 us

profile of v3, /device:TPU:0, one launch (start us, length us, event | category | flops | bytes accessed | tf_op | source)
XLA Modules:
  0.0 73.2 jit_solution(1027401852608036795)
XLA Ops:
  0.7 71.2 %shard_map.64 = f32[32,128]{1,0:T(8,128)} custom-call(bf16[1,12,512,128]{3,2,1,0:T(8,128)(2,1)} %panel.1, f32[12,1,512]{2,1,0:T(1,128)} %bitcast.1, s32[1]{0:T(128)S(6)} %copy.8.counts, s32[1,2,2048]{2,1,0:T(2,128)} %faces.1, bf16[1,12,512,512]{3,2,1,0:T(8,128)(2,1)} %stiffness.1, bf16[1,24576,256]{2,1,0:T(8,128)(2,1)} %resident.1), custom_call_target="tpu_custom_call" | custom-call | flops 2684354560 | bytes 20447232 | tf_op jit(solution)/shard_map/pallas_call | solution.py:241
  71.9 1.3 %copy.9 = f32[32,128]{1,0:T(8,128)} copy(f32[32,128]{1,0:T(8,128)} %shard_map.64) | data formatting | bytes 32768

commit v4 on v3

--- a/solution.py
+++ b/solution.py
@@ -10,6 +10,7 @@
 MESH = pl.DeviceIdType.MESH
 ROWS_FIRST = (((0,), (0,)), ((), ()))
 DEPTH = 4
+RES_DEPTH = 16
 GATHER_PIECES = 8
 GROUP = 8
 BATCH = 16
@@ -17,8 +18,8 @@
 
 def gram_kernel(
     n, panel, mass, counts, faces, stiffness, resident, out,
-    applied, res, wide, kbuf, rbuf, res_rows, picked, leaving, arrived, acc, gram, terms,
-    k_sem, r_sem, far_send, far_recv, mate_send, mate_recv, on_send, on_recv,
+    applied, res, wide, kbuf, pbuf, rbuf, res_rows, picked, leaving, arrived, acc, gram, terms,
+    k_sem, p_sem, r_sem, far_send, far_recv, mate_send, mate_recv, on_send, on_recv,
     face_send, face_recv, ffar_send, ffar_recv, fmate_send, fmate_recv, fon_send, fon_recv,
     sum_send, sum_recv,
 ):
@@ -38,16 +39,21 @@
 
     def res_copy(s):
         rows = pl.ds(pl.multiple_of(s * nodes, nodes), nodes)
-        return pltpu.make_async_copy(resident.at[0, rows], rbuf.at[lax.rem(s, DEPTH)], r_sem.at[lax.rem(s, DEPTH)])
+        return pltpu.make_async_copy(resident.at[0, rows], rbuf.at[lax.rem(s, RES_DEPTH)], r_sem.at[lax.rem(s, RES_DEPTH)])
+
+    def panel_copy(e):
+        return pltpu.make_async_copy(panel.at[0, e], pbuf.at[e], p_sem.at[e])
 
     def to(buffer, index, send, recv, k, column):
         return pltpu.make_async_remote_copy(
             src_ref=buffer.at[index], dst_ref=buffer.at[index], send_sem=send.at[k], recv_sem=recv.at[k],
             device_id=(column, me), device_id_type=MESH)
 
-    for e in range(DEPTH):
-        stiff_copy(jnp.int32(e)).start()
-    for s in range(DEPTH):
+    for e in range(slots):
+        if e < DEPTH:
+            stiff_copy(jnp.int32(e)).start()
+        panel_copy(e).start()
+    for s in range(RES_DEPTH):
         res_copy(jnp.int32(s)).start()
     barrier = pltpu.get_barrier_semaphore()
     for step in range(1, n):
@@ -65,7 +71,8 @@
 
     def apply_slot(e, carry):
         stiff_copy(e).wait()
-        values = panel[0, e]
+        panel_copy(e).wait()
+        values = pbuf[e]
         product = jnp.dot(kbuf[lax.rem(e, DEPTH)], values, preferred_element_type=jnp.float32)
         product = product + node_weights(e) * values.astype(jnp.float32)
         live = jnp.where(c * slots + e < counts[0], 1.0, 0.0)
@@ -82,21 +89,25 @@
 
     def widen_resident(s, carry):
         res_copy(s).wait()
-        res[pl.ds(pl.multiple_of(s * nodes, nodes), nodes), :] = rbuf[lax.rem(s, DEPTH)].astype(jnp.float32)
-
-        @pl.when(s + DEPTH < all_slots)
+        res[pl.ds(pl.multiple_of(s * nodes, nodes), nodes), :] = rbuf[lax.rem(s, RES_DEPTH)].astype(jnp.float32)
+
+        @pl.when(s + RES_DEPTH < all_slots)
         def _():
-            res_copy(s + DEPTH).start()
+            res_copy(s + RES_DEPTH).start()
         return carry
 
     lax.fori_loop(0, all_slots, widen_resident, 0)
 
-    def add_slot(slot):
-        rows = pl.ds(pl.multiple_of(slot * nodes, nodes), nodes)
-        block = applied[slot]
-        wide[rows, :] = block.astype(jnp.float32)
-        acc[...] += lax.dot_general(
-            block, res[rows, :].astype(jnp.bfloat16), ROWS_FIRST, preferred_element_type=jnp.float32)
+    def add_slots(*which):
+        total = None
+        for slot in which:
+            rows = pl.ds(pl.multiple_of(slot * nodes, nodes), nodes)
+            block = applied[slot]
+            wide[rows, :] = block.astype(jnp.float32)
+            term = lax.dot_general(
+                block, res[rows, :].astype(jnp.bfloat16), ROWS_FIRST, preferred_element_type=jnp.float32)
+            total = term if total is None else total + term
+        acc[...] += total
 
     def gather_rows(source, l, first, target, target_first, count):
         def groups(i, carry):
@@ -115,10 +126,9 @@
         gather_rows(res, lax.div(piece, half), lax.rem(piece, half) * piece_rows,
                     res_rows, piece * (piece_rows // GROUP), piece_rows)
 
-    def exchange_slot(e, carry):
-        add_slot(c * slots + e)
+    def near_slots(e):
         to(applied, mate * slots + e, mate_send, mate_recv, e, mate).wait_recv()
-        add_slot(mate * slots + e)
+        add_slots(c * slots + e, mate * slots + e)
 
         @pl.when(e < GATHER_PIECES)
         def _():
@@ -126,17 +136,18 @@
 
         to(applied, far * slots + e, far_send, far_recv, e, far).wait_recv()
         to(applied, far * slots + e, on_send, on_recv, e, mate).start()
-        add_slot(far * slots + e)
-
-        @pl.when(e > 0)
-        def _():
-            to(applied, opposite * slots + e - 1, on_send, on_recv, e - 1, mate).wait_recv()
-            add_slot(opposite * slots + e - 1)
-        return carry
-
-    lax.fori_loop(0, slots, exchange_slot, 0)
+
+    def exchange_slot(e, carry):
+        near_slots(e)
+        to(applied, opposite * slots + e - 1, on_send, on_recv, e - 1, mate).wait_recv()
+        add_slots(far * slots + e, opposite * slots + e - 1)
+        return carry
+
+    near_slots(jnp.int32(0))
+    add_slots(far * slots)
+    lax.fori_loop(1, slots, exchange_slot, 0)
     to(applied, opposite * slots + slots - 1, on_send, on_recv, slots - 1, mate).wait_recv()
-    add_slot(opposite * slots + slots - 1)
+    add_slots(opposite * slots + slots - 1)
 
     has = (me < n - 1, me > 0)
     target = (jnp.maximum(me - 1, 0), jnp.minimum(me + 1, n - 1))
@@ -241,14 +252,15 @@
     return pl.pallas_call(
         functools.partial(gram_kernel, n),
         out_shape=jax.ShapeDtypeStruct((own, width), f32),
-        in_specs=[vmem, vmem, smem, smem, anywhere, anywhere],
+        in_specs=[anywhere, vmem, smem, smem, anywhere, anywhere],
         out_specs=vmem,
         scratch_shapes=[
             pltpu.VMEM((columns * slots, nodes, width), bf16),
             pltpu.VMEM((rows, kept), f32),
             pltpu.VMEM((rows, width), f32),
             pltpu.VMEM((DEPTH, nodes, nodes), bf16),
-            pltpu.VMEM((DEPTH, nodes, kept), bf16),
+            pltpu.VMEM((slots, nodes, width), bf16),
+            pltpu.VMEM((RES_DEPTH, nodes, kept), bf16),
             pltpu.VMEM((2 * face_n // GROUP, GROUP, kept), f32),
             pltpu.VMEM((quarter // GROUP, GROUP, width), f32),
             pltpu.VMEM((2, quarter, width), bf16),
@@ -256,7 +268,7 @@
             pltpu.VMEM((width, kept), f32),
             pltpu.VMEM((kept, width), f32),
             pltpu.VMEM((n - 1, own, width), f32),
-            dma((DEPTH,)), dma((DEPTH,)),
+            dma((DEPTH,)), dma((slots,)), dma((RES_DEPTH,)),
             dma((slots,)), dma((slots,)), dma((slots,)), dma((slots,)), dma((slots,)), dma((slots,)),
             dma((2,)), dma((2,)), dma((2,)), dma((2,)), dma((2,)), dma((2,)), dma((2,)), dma((2,)),
             dma((n - 1,)), dma((n - 1,)),

time: 73.8 us -> 68.4 us (0.927)
  Pallas kernels: 71.2 us -> 66.1 us
    pallas_call x1, Pallas kernels: 71.2 us -> 66.1 us  [shards(): pl.pallas_call(functools.partial(gram_kernel, n), out_shape=jax.ShapeDtyp...]
where the time goes in v4:
time: 68.4 us; the launch traced here: 68.1 us
  Pallas kernels  66.1 us (97%)
  local copies, waits for them, and re-layouts  1.32 us (2%)
    pallas_call x1, Pallas kernels, shards(): pl.pallas_call(functools.partial(gram_kernel, n), out_shape=jax.ShapeDtyp...  66.1 us

profile of v4, /device:TPU:0, one launch (start us, length us, event | category | flops | bytes accessed | tf_op | source)
XLA Modules:
  0.0 68.1 jit_solution(6138670875462335750)
XLA Ops:
  0.7 66.1 %shard_map.64 = f32[32,128]{1,0:T(8,128)} custom-call(bf16[1,12,512,128]{3,2,1,0:T(8,128)(2,1)} %panel.1, f32[12,1,512]{2,1,0:T(1,128)} %bitcast.1, s32[1]{0:T(128)S(6)} %copy.8.counts, s32[1,2,2048]{2,1,0:T(2,128)} %faces.1, bf16[1,12,512,512]{3,2,1,0:T(8,128)(2,1)} %stiffness.1, bf16[1,24576,256]{2,1,0:T(8,128)(2,1)} %resident.1), custom_call_target="tpu_custom_call" | custom-call | flops 2684354560 | bytes 20447232 | tf_op jit(solution)/shard_map/pallas_call | solution.py:252
  66.7 1.3 %copy.9 = f32[32,128]{1,0:T(8,128)} copy(f32[32,128]{1,0:T(8,128)} %shard_map.64) | data formatting | bytes 32768

commit v5 on v4

--- a/solution.py
+++ b/solution.py
@@ -11,17 +11,16 @@
 ROWS_FIRST = (((0,), (0,)), ((), ()))
 DEPTH = 4
 RES_DEPTH = 16
-GATHER_PIECES = 8
+PIECES = 4
 GROUP = 8
-BATCH = 16
 
 
 def gram_kernel(
     n, panel, mass, counts, faces, stiffness, resident, out,
-    applied, res, wide, kbuf, pbuf, rbuf, res_rows, picked, leaving, arrived, acc, gram, terms,
+    applied, res, wide, kbuf, pbuf, rbuf, res_picked, res_rows, other_rows, picked, half_picked, leaving, arrived, acc, gram, terms,
     k_sem, p_sem, r_sem, far_send, far_recv, mate_send, mate_recv, on_send, on_recv,
     face_send, face_recv, ffar_send, ffar_recv, fmate_send, fmate_recv, fon_send, fon_recv,
-    sum_send, sum_recv,
+    row_send, row_recv, sum_send, sum_recv,
 ):
     me = lax.axis_index("row")
     c = lax.axis_index("col")
@@ -30,7 +29,9 @@
     opposite = (1 - c // 2) * 2 + (1 - c % 2)
     slots, nodes = panel.shape[1], panel.shape[2]
     face_n = faces.shape[2]
-    quarter = face_n // 4
+    quarter = face_n // PIECES
+    half = quarter // 2
+    following = jnp.minimum(me + 1, n - 1)
     own = out.shape[0]
     all_slots = applied.shape[0]
 
@@ -69,6 +70,14 @@
         pieces = [jnp.broadcast_to(mass[e, :, k:k + width], (width, width)).T for k in range(0, nodes, width)]
         return jnp.concatenate(pieces, axis=0)
 
+    def widen_resident(s):
+        res_copy(s).wait()
+        res[pl.ds(pl.multiple_of(s * nodes, nodes), nodes), :] = rbuf[lax.rem(s, RES_DEPTH)].astype(jnp.float32)
+
+        @pl.when(s + RES_DEPTH < all_slots)
+        def _():
+            res_copy(s + RES_DEPTH).start()
+
     def apply_slot(e, carry):
         stiff_copy(e).wait()
         panel_copy(e).wait()
@@ -83,20 +92,12 @@
         @pl.when(e + DEPTH < slots)
         def _():
             stiff_copy(e + DEPTH).start()
+
+        for t in range(all_slots // slots):
+            widen_resident(e * (all_slots // slots) + t)
         return carry
 
     lax.fori_loop(0, slots, apply_slot, 0)
-
-    def widen_resident(s, carry):
-        res_copy(s).wait()
-        res[pl.ds(pl.multiple_of(s * nodes, nodes), nodes), :] = rbuf[lax.rem(s, RES_DEPTH)].astype(jnp.float32)
-
-        @pl.when(s + RES_DEPTH < all_slots)
-        def _():
-            res_copy(s + RES_DEPTH).start()
-        return carry
-
-    lax.fori_loop(0, all_slots, widen_resident, 0)
 
     def add_slots(*which):
         total = None
@@ -109,28 +110,35 @@
             total = term if total is None else total + term
         acc[...] += total
 
-    def gather_rows(source, l, first, target, target_first, count):
+    def gather_rows(source, l, first, target, count, batch):
         def groups(i, carry):
-            base = pl.multiple_of(first + i * BATCH, BATCH)
-            rows = [faces[0, l, base + t] for t in range(BATCH)]
+            base = pl.multiple_of(first + i * batch, batch)
+            rows = [faces[0, l, base + t] for t in range(batch)]
             values = [source[pl.ds(row, 1), :] for row in rows]
             for t, value in enumerate(values):
-                target[target_first + i * (BATCH // GROUP) + t // GROUP, t % GROUP:t % GROUP + 1, :] = value
+                target[i * (batch // GROUP) + t // GROUP, t % GROUP:t % GROUP + 1, :] = value
             return carry
-        lax.fori_loop(0, count // BATCH, groups, 0)
-
-    piece_rows = 2 * face_n // GATHER_PIECES
-    half = GATHER_PIECES // 2
+        lax.fori_loop(0, count // batch, groups, 0)
+
+    def row_copy(piece):
+        return pltpu.make_async_remote_copy(
+            src_ref=res_rows.at[piece], dst_ref=other_rows.at[piece],
+            send_sem=row_send.at[piece], recv_sem=row_recv.at[piece],
+            device_id=(c, following), device_id_type=MESH)
 
     def gather_resident(piece):
-        gather_rows(res, lax.div(piece, half), lax.rem(piece, half) * piece_rows,
-                    res_rows, piece * (piece_rows // GROUP), piece_rows)
+        gather_rows(res, 1 - lax.div(piece, PIECES), lax.rem(piece, PIECES) * quarter, res_picked, quarter, 16)
+        res_rows[piece] = res_picked[...].reshape(quarter, res_picked.shape[2]).astype(jnp.bfloat16)
+
+        @pl.when(jnp.logical_and(piece < PIECES, me < n - 1))
+        def _():
+            row_copy(piece).start()
 
     def near_slots(e):
         to(applied, mate * slots + e, mate_send, mate_recv, e, mate).wait_recv()
         add_slots(c * slots + e, mate * slots + e)
 
-        @pl.when(e < GATHER_PIECES)
+        @pl.when(e < 2 * PIECES)
         def _():
             gather_resident(e)
 
@@ -149,57 +157,53 @@
     to(applied, opposite * slots + slots - 1, on_send, on_recv, slots - 1, mate).wait_recv()
     add_slots(opposite * slots + slots - 1)
 
-    has = (me < n - 1, me > 0)
-    target = (jnp.maximum(me - 1, 0), jnp.minimum(me + 1, n - 1))
-    sends = (me > 0, me < n - 1)
-
-    def face_copy(l):
+    def face_copy(h):
         return pltpu.make_async_remote_copy(
-            src_ref=leaving.at[l], dst_ref=arrived.at[l, c], send_sem=face_send.at[l], recv_sem=face_recv.at[l],
-            device_id=(c, target[l]), device_id_type=MESH)
-
-    for l in range(2):
-        gather_rows(wide, l, c * quarter, picked, 0, quarter)
-        leaving[l] = picked[...].reshape(quarter, picked.shape[2]).astype(jnp.bfloat16)
-
-        @pl.when(sends[l])
-        def _(l=l):
-            face_copy(l).start()
-
-    def share(l, column, send, recv, to_column):
+            src_ref=leaving.at[h], dst_ref=arrived.at[h, c], send_sem=face_send.at[h], recv_sem=face_recv.at[h],
+            device_id=(c, following), device_id_type=MESH)
+
+    def share(h, column, send, recv, to_column):
         return pltpu.make_async_remote_copy(
-            src_ref=arrived.at[l, column], dst_ref=arrived.at[l, column], send_sem=send.at[l], recv_sem=recv.at[l],
+            src_ref=arrived.at[h, column], dst_ref=arrived.at[h, column], send_sem=send.at[h], recv_sem=recv.at[h],
             device_id=(to_column, me), device_id_type=MESH)
 
-    def add_face(l, column):
-        groups = quarter // GROUP
-        start = (1 - l) * (face_n // GROUP) + column * groups
-        rows = res_rows[pl.ds(start, groups)].reshape(quarter, res_rows.shape[2])
+    def add_face(h, column):
         acc[...] += lax.dot_general(
-            arrived[l, column], rows.astype(jnp.bfloat16), ROWS_FIRST, preferred_element_type=jnp.float32)
-
-    for l in range(2):
-        @pl.when(has[l])
-        def _(l=l):
-            face_copy(l).wait_recv()
-
-        @pl.when(jnp.logical_not(has[l]))
-        def _(l=l):
-            arrived[l, c] = jnp.zeros(arrived.shape[2:], jnp.bfloat16)
-
-        share(l, c, ffar_send, ffar_recv, far).start()
-        share(l, c, fmate_send, fmate_recv, mate).start()
-    for l in range(2):
-        add_face(l, c)
-        share(l, mate, fmate_send, fmate_recv, mate).wait_recv()
-        add_face(l, mate)
-    for l in range(2):
-        share(l, far, ffar_send, ffar_recv, far).wait_recv()
-        share(l, far, fon_send, fon_recv, mate).start()
-        add_face(l, far)
-    for l in range(2):
-        share(l, opposite, fon_send, fon_recv, mate).wait_recv()
-        add_face(l, opposite)
+            arrived[h, column], res_rows[PIECES + column, h * half:(h + 1) * half], ROWS_FIRST,
+            preferred_element_type=jnp.float32)
+
+    def add_other(piece):
+        gather_rows(wide, 0, piece * quarter, picked, quarter, 32)
+        row_copy(jnp.int32(piece)).wait_recv()
+        block = picked[...].reshape(quarter, picked.shape[2]).astype(jnp.bfloat16)
+        acc[...] += lax.dot_general(block, other_rows[piece], ROWS_FIRST, preferred_element_type=jnp.float32)
+
+    @pl.when(me < n - 1)
+    def _():
+        for h in range(2):
+            gather_rows(wide, 1, c * quarter + h * half, half_picked, half, 32)
+            leaving[h] = half_picked[...].reshape(half, half_picked.shape[2]).astype(jnp.bfloat16)
+            face_copy(h).start()
+
+    @pl.when(me > 0)
+    def _():
+        for h in range(2):
+            add_other(h)
+            face_copy(h).wait_recv()
+            share(h, c, ffar_send, ffar_recv, far).start()
+            share(h, c, fmate_send, fmate_recv, mate).start()
+        for h in range(2):
+            add_other(2 + h)
+            share(h, far, ffar_send, ffar_recv, far).wait_recv()
+            share(h, far, fon_send, fon_recv, mate).start()
+        for h in range(2):
+            add_face(h, c)
+            add_face(h, far)
+            share(h, mate, fmate_send, fmate_recv, mate).wait_recv()
+            add_face(h, mate)
+        for h in range(2):
+            share(h, opposite, fon_send, fon_recv, mate).wait_recv()
+            add_face(h, opposite)
 
     gram[...] = acc[...].T
     copies = []
@@ -219,13 +223,21 @@
         return carry
 
     lax.fori_loop(0, slots, drain, 0)
-    for l in range(2):
-        @pl.when(sends[l])
-        def _(l=l):
-            face_copy(l).wait_send()
-        share(l, c, ffar_send, ffar_recv, far).wait_send()
-        share(l, c, fmate_send, fmate_recv, mate).wait_send()
-        share(l, far, fon_send, fon_recv, mate).wait_send()
+
+    @pl.when(me < n - 1)
+    def _():
+        for h in range(2):
+            face_copy(h).wait_send()
+        for piece in range(PIECES):
+            row_copy(jnp.int32(piece)).wait_send()
+
+    @pl.when(me > 0)
+    def _():
+        for h in range(2):
+            share(h, c, ffar_send, ffar_recv, far).wait_send()
+            share(h, c, fmate_send, fmate_recv, mate).wait_send()
+            share(h, far, fon_send, fon_recv, mate).wait_send()
+
     total = gram[pl.ds(pl.multiple_of(me * own, own), own), :]
     for step, copy in enumerate(copies):
         copy.wait_recv()
@@ -261,17 +273,20 @@
             pltpu.VMEM((DEPTH, nodes, nodes), bf16),
             pltpu.VMEM((slots, nodes, width), bf16),
             pltpu.VMEM((RES_DEPTH, nodes, kept), bf16),
-            pltpu.VMEM((2 * face_n // GROUP, GROUP, kept), f32),
+            pltpu.VMEM((quarter // GROUP, GROUP, kept), f32),
+            pltpu.VMEM((2 * PIECES, quarter, kept), bf16),
+            pltpu.VMEM((PIECES, quarter, kept), bf16),
             pltpu.VMEM((quarter // GROUP, GROUP, width), f32),
-            pltpu.VMEM((2, quarter, width), bf16),
-            pltpu.VMEM((2, columns, quarter, width), bf16),
+            pltpu.VMEM((quarter // 2 // GROUP, GROUP, width), f32),
+            pltpu.VMEM((2, quarter // 2, width), bf16),
+            pltpu.VMEM((2, columns, quarter // 2, width), bf16),
             pltpu.VMEM((width, kept), f32),
             pltpu.VMEM((kept, width), f32),
             pltpu.VMEM((n - 1, own, width), f32),
             dma((DEPTH,)), dma((slots,)), dma((RES_DEPTH,)),
             dma((slots,)), dma((slots,)), dma((slots,)), dma((slots,)), dma((slots,)), dma((slots,)),
             dma((2,)), dma((2,)), dma((2,)), dma((2,)), dma((2,)), dma((2,)), dma((2,)), dma((2,)),
-            dma((n - 1,)), dma((n - 1,)),
+            dma((PIECES,)), dma((PIECES,)), dma((n - 1,)), dma((n - 1,)),
         ],
         compiler_params=pltpu.CompilerParams(
             collective_id=0, has_side_effects=True, vmem_limit_bytes=62 * 1024 * 1024),

time: 68.4 us -> 62.1 us (0.908)
  Pallas kernels: 66.1 us -> 59.7 us
    pallas_call x1, Pallas kernels: 66.1 us -> 59.7 us  [shards(): pl.pallas_call(functools.partial(gram_kernel, n), out_shape=jax.ShapeDtyp...]
where the time goes in v5:
time: 62.1 us; the launch traced here: 61.7 us
  Pallas kernels  59.7 us (96%)
  local copies, waits for them, and re-layouts  1.32 us (2%)
  between operations  0.66 us (1%)
    pallas_call x1, Pallas kernels, shards(): pl.pallas_call(functools.partial(gram_kernel, n), out_shape=jax.ShapeDtyp...  59.7 us
    unnamed x1, local copies, waits for them, and re-layouts  1.32 us

profile of v5, /device:TPU:0, one launch (start us, length us, event | category | flops | bytes accessed | tf_op | source)
XLA Modules:
  0.0 61.7 jit_solution(12761275070461936025)
XLA Ops:
  0.7 59.7 %shard_map.64 = f32[32,128]{1,0:T(8,128)} custom-call(bf16[1,12,512,128]{3,2,1,0:T(8,128)(2,1)} %panel.1, f32[12,1,512]{2,1,0:T(1,128)} %bitcast.1, s32[1]{0:T(128)S(6)} %copy.8.counts, s32[1,2,2048]{2,1,0:T(2,128)} %faces.1, bf16[1,12,512,512]{3,2,1,0:T(8,128)(2,1)} %stiffness.1, bf16[1,24576,256]{2,1,0:T(8,128)(2,1)} %resident.1), custom_call_target="tpu_custom_call" | custom-call | flops 2684354560 | bytes 20447232 | tf_op jit(solution)/shard_map/pallas_call | solution.py:264
  60.4 1.3 %copy.9 = f32[32,128]{1,0:T(8,128)} copy(f32[32,128]{1,0:T(8,128)} %shard_map.64) | data formatting | bytes 32768

commit v6 on v5

--- a/solution.py
+++ b/solution.py
@@ -17,10 +17,10 @@
 
 def gram_kernel(
     n, panel, mass, counts, faces, stiffness, resident, out,
-    applied, res, wide, kbuf, pbuf, rbuf, res_picked, res_rows, other_rows, picked, half_picked, leaving, arrived, acc, gram, terms,
+    applied, res, wide, kbuf, pbuf, rbuf, res_picked, res_rows, other_rows, picked, half_picked, near_rows, leaving, arrived, acc, gram, terms,
     k_sem, p_sem, r_sem, far_send, far_recv, mate_send, mate_recv, on_send, on_recv,
     face_send, face_recv, ffar_send, ffar_recv, fmate_send, fmate_recv, fon_send, fon_recv,
-    row_send, row_recv, sum_send, sum_recv,
+    row_send, row_recv, near_send, near_recv, sum_send, sum_recv,
 ):
     me = lax.axis_index("row")
     c = lax.axis_index("col")
@@ -127,7 +127,7 @@
             device_id=(c, following), device_id_type=MESH)
 
     def gather_resident(piece):
-        gather_rows(res, 1 - lax.div(piece, PIECES), lax.rem(piece, PIECES) * quarter, res_picked, quarter, 16)
+        gather_rows(res, 1 - lax.div(piece, PIECES), lax.rem(piece, PIECES) * quarter, res_picked, quarter, 32)
         res_rows[piece] = res_picked[...].reshape(quarter, res_picked.shape[2]).astype(jnp.bfloat16)
 
         @pl.when(jnp.logical_and(piece < PIECES, me < n - 1))
@@ -157,26 +157,39 @@
     to(applied, opposite * slots + slots - 1, on_send, on_recv, slots - 1, mate).wait_recv()
     add_slots(opposite * slots + slots - 1)
 
+    def halves(h):
+        return pl.ds(h * half, half)
+
     def face_copy(h):
         return pltpu.make_async_remote_copy(
-            src_ref=leaving.at[h], dst_ref=arrived.at[h, c], send_sem=face_send.at[h], recv_sem=face_recv.at[h],
-            device_id=(c, following), device_id_type=MESH)
+            src_ref=leaving.at[h], dst_ref=arrived.at[c, halves(h)], send_sem=face_send.at[h],
+            recv_sem=face_recv.at[h], device_id=(c, following), device_id_type=MESH)
 
     def share(h, column, send, recv, to_column):
-        return pltpu.make_async_remote_copy(
-            src_ref=arrived.at[h, column], dst_ref=arrived.at[h, column], send_sem=send.at[h], recv_sem=recv.at[h],
-            device_id=(to_column, me), device_id_type=MESH)
-
-    def add_face(h, column):
-        acc[...] += lax.dot_general(
-            arrived[h, column], res_rows[PIECES + column, h * half:(h + 1) * half], ROWS_FIRST,
-            preferred_element_type=jnp.float32)
-
-    def add_other(piece):
-        gather_rows(wide, 0, piece * quarter, picked, quarter, 32)
-        row_copy(jnp.int32(piece)).wait_recv()
-        block = picked[...].reshape(quarter, picked.shape[2]).astype(jnp.bfloat16)
-        acc[...] += lax.dot_general(block, other_rows[piece], ROWS_FIRST, preferred_element_type=jnp.float32)
+        return to(arrived, (column, halves(h)), send, recv, h, to_column)
+
+    def add_products(*pairs):
+        total = None
+        for left, right in pairs:
+            term = lax.dot_general(left, right, ROWS_FIRST, preferred_element_type=jnp.float32)
+            total = term if total is None else total + term
+        acc[...] += total
+
+    def face_pair(column):
+        return arrived[column], res_rows[PIECES + column]
+
+    def other_pair(piece):
+        return near_rows[piece], other_rows[piece]
+
+    mine, others = (c % 2) * (PIECES // 2), (1 - c % 2) * (PIECES // 2)
+
+    def near_copy(k, first):
+        return to(near_rows, first + k, near_send, near_recv, k, mate)
+
+    def pick_near(k):
+        gather_rows(wide, 0, (mine + k) * quarter, picked, quarter, 32)
+        near_rows[mine + k] = picked[...].reshape(quarter, picked.shape[2]).astype(jnp.bfloat16)
+        near_copy(k, mine).start()
 
     @pl.when(me < n - 1)
     def _():
@@ -188,22 +201,26 @@
     @pl.when(me > 0)
     def _():
         for h in range(2):
-            add_other(h)
+            pick_near(h)
             face_copy(h).wait_recv()
             share(h, c, ffar_send, ffar_recv, far).start()
             share(h, c, fmate_send, fmate_recv, mate).start()
-        for h in range(2):
-            add_other(2 + h)
+        for piece in range(PIECES):
+            row_copy(jnp.int32(piece)).wait_recv()
+        add_products(other_pair(mine), other_pair(mine + 1))
+        for h in range(2):
             share(h, far, ffar_send, ffar_recv, far).wait_recv()
             share(h, far, fon_send, fon_recv, mate).start()
-        for h in range(2):
-            add_face(h, c)
-            add_face(h, far)
+            if h == 0:
+                for k in range(2):
+                    near_copy(k, others).wait_recv()
+                add_products(other_pair(others), other_pair(others + 1))
+        for h in range(2):
             share(h, mate, fmate_send, fmate_recv, mate).wait_recv()
-            add_face(h, mate)
+        add_products(face_pair(c), face_pair(far), face_pair(mate))
         for h in range(2):
             share(h, opposite, fon_send, fon_recv, mate).wait_recv()
-            add_face(h, opposite)
+        add_products(face_pair(opposite))
 
     gram[...] = acc[...].T
     copies = []
@@ -237,6 +254,7 @@
             share(h, c, ffar_send, ffar_recv, far).wait_send()
             share(h, c, fmate_send, fmate_recv, mate).wait_send()
             share(h, far, fon_send, fon_recv, mate).wait_send()
+            near_copy(h, mine).wait_send()
 
     total = gram[pl.ds(pl.multiple_of(me * own, own), own), :]
     for step, copy in enumerate(copies):
@@ -278,15 +296,16 @@
             pltpu.VMEM((PIECES, quarter, kept), bf16),
             pltpu.VMEM((quarter // GROUP, GROUP, width), f32),
             pltpu.VMEM((quarter // 2 // GROUP, GROUP, width), f32),
+            pltpu.VMEM((PIECES, quarter, width), bf16),
             pltpu.VMEM((2, quarter // 2, width), bf16),
-            pltpu.VMEM((2, columns, quarter // 2, width), bf16),
+            pltpu.VMEM((columns, quarter, width), bf16),
             pltpu.VMEM((width, kept), f32),
             pltpu.VMEM((kept, width), f32),
             pltpu.VMEM((n - 1, own, width), f32),
             dma((DEPTH,)), dma((slots,)), dma((RES_DEPTH,)),
             dma((slots,)), dma((slots,)), dma((slots,)), dma((slots,)), dma((slots,)), dma((slots,)),
             dma((2,)), dma((2,)), dma((2,)), dma((2,)), dma((2,)), dma((2,)), dma((2,)), dma((2,)),
-            dma((PIECES,)), dma((PIECES,)), dma((n - 1,)), dma((n - 1,)),
+            dma((PIECES,)), dma((PIECES,)), dma((2,)), dma((2,)), dma((n - 1,)), dma((n - 1,)),
         ],
         compiler_params=pltpu.CompilerParams(
             collective_id=0, has_side_effects=True, vmem_limit_bytes=62 * 1024 * 1024),

time: 62.1 us -> 62.1 us (level)
  no operation moved by 1% of the time
where the time goes in v6:
time: 62.1 us; the launch traced here: 61.8 us
  Pallas kernels  59.8 us (96%)
  local copies, waits for them, and re-layouts  1.32 us (2%)
  between operations  0.66 us (1%)
    pallas_call x1, Pallas kernels, shards(): pl.pallas_call(functools.partial(gram_kernel, n), out_shape=jax.ShapeDtyp...  59.8 us
    unnamed x1, local copies, waits for them, and re-layouts  1.32 us

profile of v6, /device:TPU:0, one launch (start us, length us, event | category | flops | bytes accessed | tf_op | source)
XLA Modules:
  0.0 61.8 jit_solution(17446811128996692968)
XLA Ops:
  0.7 59.8 %shard_map.64 = f32[32,128]{1,0:T(8,128)} custom-call(bf16[1,12,512,128]{3,2,1,0:T(8,128)(2,1)} %panel.1, f32[12,1,512]{2,1,0:T(1,128)} %bitcast.1, s32[1]{0:T(128)S(6)} %copy.8.counts, s32[1,2,2048]{2,1,0:T(2,128)} %faces.1, bf16[1,12,512,512]{3,2,1,0:T(8,128)(2,1)} %stiffness.1, bf16[1,24576,256]{2,1,0:T(8,128)(2,1)} %resident.1), custom_call_target="tpu_custom_call" | custom-call | flops 2684354560 | bytes 20447232 | tf_op jit(solution)/shard_map/pallas_call | solution.py:282
  60.5 1.3 %copy.9 = f32[32,128]{1,0:T(8,128)} copy(f32[32,128]{1,0:T(8,128)} %shard_map.64) | data formatting | bytes 32768

commit v7 on v6

--- a/solution.py
+++ b/solution.py
@@ -12,6 +12,7 @@
 DEPTH = 4
 RES_DEPTH = 16
 PIECES = 4
+AHEAD = 6
 GROUP = 8
 
 
@@ -86,7 +87,10 @@
         product = product + node_weights(e) * values.astype(jnp.float32)
         live = jnp.where(c * slots + e < counts[0], 1.0, 0.0)
         applied[c * slots + e] = (product * live).astype(jnp.bfloat16)
-        to(applied, c * slots + e, far_send, far_recv, e, far).start()
+
+        @pl.when(e < AHEAD)
+        def _():
+            to(applied, c * slots + e, far_send, far_recv, e, far).start()
         to(applied, c * slots + e, mate_send, mate_recv, e, mate).start()
 
         @pl.when(e + DEPTH < slots)
@@ -144,6 +148,10 @@
 
         to(applied, far * slots + e, far_send, far_recv, e, far).wait_recv()
         to(applied, far * slots + e, on_send, on_recv, e, mate).start()
+
+        @pl.when(e + AHEAD < slots)
+        def _():
+            to(applied, c * slots + e + AHEAD, far_send, far_recv, e + AHEAD, far).start()
 
     def exchange_slot(e, carry):
         near_slots(e)

time: 62.1 us -> 62.1 us (level)
  no operation moved by 1% of the time
where the time goes in v7:
time: 62.1 us; the launch traced here: 61.8 us
  Pallas kernels  59.8 us (96%)
  local copies, waits for them, and re-layouts  1.32 us (2%)
  between operations  0.66 us (1%)
    pallas_call x1, Pallas kernels, shards(): pl.pallas_call(functools.partial(gram_kernel, n), out_shape=jax.ShapeDtyp...  59.8 us
    unnamed x1, local copies, waits for them, and re-layouts  1.32 us

profile of v7, /device:TPU:0, one launch (start us, length us, event | category | flops | bytes accessed | tf_op | source)
XLA Modules:
  0.0 61.8 jit_solution(10960409869719382490)
XLA Ops:
  0.7 59.8 %shard_map.64 = f32[32,128]{1,0:T(8,128)} custom-call(bf16[1,12,512,128]{3,2,1,0:T(8,128)(2,1)} %panel.1, f32[12,1,512]{2,1,0:T(1,128)} %bitcast.1, s32[1]{0:T(128)S(6)} %copy.8.counts, s32[1,2,2048]{2,1,0:T(2,128)} %faces.1, bf16[1,12,512,512]{3,2,1,0:T(8,128)(2,1)} %stiffness.1, bf16[1,24576,256]{2,1,0:T(8,128)(2,1)} %resident.1), custom_call_target="tpu_custom_call" | custom-call | flops 2684354560 | bytes 20447232 | tf_op jit(solution)/shard_map/pallas_call | solution.py:290
  60.5 1.3 %copy.9 = f32[32,128]{1,0:T(8,128)} copy(f32[32,128]{1,0:T(8,128)} %shard_map.64) | data formatting | bytes 32768

commit v8 on v7

--- a/solution.py
+++ b/solution.py
@@ -138,14 +138,7 @@
         def _():
             row_copy(piece).start()
 
-    def near_slots(e):
-        to(applied, mate * slots + e, mate_send, mate_recv, e, mate).wait_recv()
-        add_slots(c * slots + e, mate * slots + e)
-
-        @pl.when(e < 2 * PIECES)
-        def _():
-            gather_resident(e)
-
+    def far_slot(e):
         to(applied, far * slots + e, far_send, far_recv, e, far).wait_recv()
         to(applied, far * slots + e, on_send, on_recv, e, mate).start()
 
@@ -153,14 +146,20 @@
         def _():
             to(applied, c * slots + e + AHEAD, far_send, far_recv, e + AHEAD, far).start()
 
+        @pl.when(e < 2 * PIECES)
+        def _():
+            gather_resident(e)
+
+        to(applied, mate * slots + e, mate_send, mate_recv, e, mate).wait_recv()
+
     def exchange_slot(e, carry):
-        near_slots(e)
+        far_slot(e)
         to(applied, opposite * slots + e - 1, on_send, on_recv, e - 1, mate).wait_recv()
-        add_slots(far * slots + e, opposite * slots + e - 1)
+        add_slots(c * slots + e, mate * slots + e, far * slots + e, opposite * slots + e - 1)
         return carry
 
-    near_slots(jnp.int32(0))
-    add_slots(far * slots)
+    far_slot(jnp.int32(0))
+    add_slots(c * slots, mate * slots, far * slots)
     lax.fori_loop(1, slots, exchange_slot, 0)
     to(applied, opposite * slots + slots - 1, on_send, on_recv, slots - 1, mate).wait_recv()
     add_slots(opposite * slots + slots - 1)

time: 62.1 us -> 62.4 us (level)
  no operation moved by 1% of the time
where the time goes in v8:
time: 62.4 us; the launch traced here: 62 us
  Pallas kernels  60 us (96%)
  local copies, waits for them, and re-layouts  1.32 us (2%)
  between operations  0.66 us (1%)
    pallas_call x1, Pallas kernels, shards(): pl.pallas_call(functools.partial(gram_kernel, n), out_shape=jax.ShapeDtyp...  60 us
    unnamed x1, local copies, waits for them, and re-layouts  1.32 us

profile of v8, /device:TPU:0, one launch (start us, length us, event | category | flops | bytes accessed | tf_op | source)
XLA Modules:
  0.0 62.0 jit_solution(11519556160081201728)
XLA Ops:
  0.7 60.0 %shard_map.64 = f32[32,128]{1,0:T(8,128)} custom-call(bf16[1,12,512,128]{3,2,1,0:T(8,128)(2,1)} %panel.1, f32[12,1,512]{2,1,0:T(1,128)} %bitcast.1, s32[1]{0:T(128)S(6)} %copy.8.counts, s32[1,2,2048]{2,1,0:T(2,128)} %faces.1, bf16[1,12,512,512]{3,2,1,0:T(8,128)(2,1)} %stiffness.1, bf16[1,24576,256]{2,1,0:T(8,128)(2,1)} %resident.1), custom_call_target="tpu_custom_call" | custom-call | flops 2684354560 | bytes 20447232 | tf_op jit(solution)/shard_map/pallas_call | solution.py:289
  60.7 1.3 %copy.9 = f32[32,128]{1,0:T(8,128)} copy(f32[32,128]{1,0:T(8,128)} %shard_map.64) | data formatting | bytes 32768
